TPU v7x, 32 devices: a whole 2x2x4 slice. The times are simulated.
32 devices in a mesh: gx: 16 (over z, y, x), gy: 2 (over core).
Axes of the slice: x: 2, y: 2, z: 4, core: 2. Of those that a mesh axis runs over, the one named last changes fastest.
Arguments:
- positions: float32 [3, 2, 139264], P(None, 'gy', 'gx'), may hold values from -7 to 7
- forces: float32 [3, 2, 139264], P(None, 'gy', 'gx'), may hold values from -6 to 6
- deriv_mat: float32 [544, 544], replicated, may hold values from -0.25 to 0.25
- quad_mat: float32 [544, 544], replicated, may hold values from -0.25 to 0.25
- point_dest: int32 [2, 139264], P('gy', 'gx'), may hold values from 0 to 32767, as said below
- leaf_center: float32 [3, 2, 4096], P(None, 'gy', 'gx'), may hold values from -4 to 4
- tile_src: int32 [2, 524288], P('gy', 'gx'), may hold values from 0 to 32768, as said below
- neighbours: int32 [2, 3, 4096], P('gy', None, 'gx'), may hold values from 0 to 4095, as said below
- inter_leaf: int32 [2, 8, 4096], P('gy', None, 'gx'), may hold values from 0 to 4095, as said below
- inter_op: int32 [2, 8, 4096], P('gy', None, 'gx'), may hold values from 0 to 15
- coarse_op: int32 [2, 16, 32], P('gy', 'gx'), may hold values from 0 to 16, as said below
- up_pinv: float32 [168, 168], replicated, may hold values from -0.5 to 0.5
- trans_ops: float32 [16, 168, 168], replicated, may hold values from -0.25 to 0.25
- child_ops: float32 [8, 168, 168], replicated, may hold values from -0.03125 to 0.03125
Outputs:
- velocity: float32 [3, 2, 139264], P(None, 'gy', 'gx')
Inputs may be any that keep to these rules, and one draw needn't show every extreme that they name: `point_dest`: within one slab and one column block d, the values are distinct; the slots sent to each owner are used from k = 0 without gaps; every column block fills all 2048 slots of the same 16 // 8 owners. `tile_src`: each point of the slab fills exactly one leaf slot of the owner it is sent to; 32768 marks an empty slot; the busiest owners have all slots filled. `neighbours`: entry 0 is the leaf itself; the others lie within 256 leaves of it. `inter_leaf`: every entry lies within 256 leaves of its leaf. `coarse_op`: 16 marks no interaction; it stands exactly for the target box itself and the boxes of the owners next to it in the same slab.
All inputs are finite; a program needn't handle non-finite values.
Results may differ from a plain program's by a relative error of at most 0.0003.
Values sent between devices are 32-bit elements; how exact they have to be, the bound alone decides.
A program may use at most 192 MiB of HBM per device.

v0:
```python
import math

import jax
import jax.numpy as jnp
from jax import lax
from jax.sharding import PartitionSpec as P

P_SIZE = 544
NOPS = 16
TILE = 128
L_DEV = 256


SOFTENING = 0.25
RADIUS = 2.5
HIGHEST = lax.Precision.HIGHEST


def extended_2(shard, sides, width):
    for axis, dim in sides:
        devices, length = (lax.axis_size(axis), shard.shape[dim])
        up = [(i, (i + 1) % devices) for i in range(devices - 1)]
        down = [(j, i) for i, j in up]
        last = lax.slice_in_dim(shard, length - width, length, axis=dim)
        first = lax.slice_in_dim(shard, 0, width, axis=dim)
        before = lax.ppermute(last, axis, up)
        after = lax.ppermute(first, axis, down)
        shard = jnp.concatenate([before, shard, after], axis=dim)
    return shard


def sphere_points(count):
    index = jnp.arange(count).astype(jnp.float32)
    height = 1.0 - (2.0 * index + 1.0) / count
    radial = jnp.sqrt(1.0 - height * height)
    angle = 2.399963 * index
    return jnp.stack([radial * jnp.cos(angle), radial * jnp.sin(angle), height])


def stokes_sum(targets, sources, strengths):
    delta_x = targets[0][:, :, None] - sources[0][:, None, :]
    delta_y = targets[1][:, :, None] - sources[1][:, None, :]
    delta_z = targets[2][:, :, None] - sources[2][:, None, :]
    soft_sq = delta_x * delta_x + delta_y * delta_y + delta_z * delta_z + SOFTENING
    inverse = 1.0 / (soft_sq * jnp.sqrt(soft_sq))
    push_x = strengths[0][:, None, :]
    push_y = strengths[1][:, None, :]
    push_z = strengths[2][:, None, :]
    projected = (push_x * delta_x + push_y * delta_y + push_z * delta_z) * inverse
    direct = (soft_sq + SOFTENING) * inverse
    return jnp.stack(
        [
            jnp.sum(push_x * direct + projected * delta_x, axis=2),
            jnp.sum(push_y * direct + projected * delta_y, axis=2),
            jnp.sum(push_z * direct + projected * delta_z, axis=2),
        ]
    )


def by_blocks(func, arrays, total, width):

    def one_block(start):
        return func(*[lax.dynamic_slice_in_dim(item, start, width, 1) for item in arrays])

    starts = jnp.arange(total // width) * width
    result = lax.map(one_block, starts)
    return jnp.transpose(result, (1, 0, 2, 3)).reshape(result.shape[1], total, result.shape[3])


def moments(tiles, centers, sphere, up_pinv, width):
    total = centers.shape[1]
    checks = centers[:, :, None] + RADIUS * sphere[:, None, :]
    values = by_blocks(stokes_sum, [checks, tiles[:3], tiles[3:]], total, width)
    stacked = jnp.transpose(values, (0, 2, 1)).reshape(-1, total)
    return jnp.dot(up_pinv.T, stacked, precision=HIGHEST, preferred_element_type=jnp.float32)


def children(multipole, child_ops):
    expansion = multipole.shape[0]
    grouped = jnp.sum(multipole.reshape(expansion, -1, L_DEV // 8, 8), axis=2)
    return jnp.einsum("cef,ebc->bf", child_ops, grouped, precision=HIGHEST)


def coarse_terms(op_rows, coarse):
    onehot = (op_rows[:, :, None] == jnp.arange(NOPS)[None, None, :]).astype(jnp.float32)
    return jnp.einsum("tbk,be->tke", onehot, coarse, precision=HIGHEST)


def translate(trans_ops, grouped):
    return jnp.einsum("kef,tke->tf", trans_ops, grouped, precision=HIGHEST)


def leaf_translate(extended, index, op_rows, trans_ops):
    picked = extended[:, index]
    onehot = (op_rows[:, :, None] == jnp.arange(NOPS)[None, None, :]).astype(jnp.float32)
    grouped = jnp.einsum("ejn,jnk->ken", picked, onehot, precision=HIGHEST)
    return jnp.einsum("kef,ken->fn", trans_ops, grouped, precision=HIGHEST)


def downward(coarse_local, child_ops, leaves):
    pushed = jnp.einsum("cfe,be->fbc", child_ops, coarse_local, precision=HIGHEST)
    expansion = pushed.shape[0]
    boxes = pushed.shape[1]
    spread = jnp.broadcast_to(pushed[:, :, None, :], (expansion, boxes, leaves // 8, 8))
    return spread.reshape(expansion, boxes * leaves)


def evaluate(tiles, centers, sphere, local, width):
    total = centers.shape[1]
    surface = centers[:, :, None] + RADIUS * sphere[:, None, :]
    density = jnp.transpose(local.reshape(3, -1, total), (0, 2, 1))
    return by_blocks(stokes_sum, [tiles[:3], surface, density], total, width)


def pick_slots(arrived, table):
    flat = arrived.reshape(arrived.shape[0], -1)
    rows_view = jnp.concatenate([flat.T, jnp.zeros((1, flat.shape[0]), jnp.float32)], axis=0)
    return jnp.take(rows_view, table, axis=0).T


def place_rows(values, where, length):
    rows_view = jnp.zeros((length + 1, values.shape[0]), jnp.float32).at[where].set(values.T)
    return rows_view[:length].T


def body(
    positions,
    forces,
    deriv_mat,
    quad_mat,
    point_dest,
    leaf_center,
    tile_src,
    neighbours,
    inter_leaf,
    inter_op,
    coarse_op,
    up_pinv,
    trans_ops,
    child_ops,
):
    owners = lax.axis_size("gx")
    count = positions.shape[2]
    leaves = leaf_center.shape[2]
    slots = leaves * TILE
    capacity = slots // owners
    tangent = jnp.dot(
        positions.reshape(-1, P_SIZE),
        deriv_mat,
        precision=HIGHEST,
        preferred_element_type=jnp.float32,
    ).reshape(3, count)
    jacobian = jnp.sqrt(1.0 + jnp.sum(tangent * tangent, axis=0))
    weighted = jnp.dot(
        forces.reshape(-1, P_SIZE), quad_mat, precision=HIGHEST, preferred_element_type=jnp.float32
    ).reshape(3, count)
    packed = jnp.concatenate([positions.reshape(3, count), weighted * jacobian[None]], axis=0)
    outgoing = place_rows(packed, point_dest[0], owners * capacity).reshape(6, owners, capacity)
    first = lax.axis_index("gx") * leaves - leaves
    arrived = lax.all_to_all(outgoing, "gx", split_axis=1, concat_axis=1, tiled=True)
    owned = pick_slots(arrived, tile_src[0])
    extended = extended_2(owned, (("gx", 1),), slots)
    sphere = sphere_points(up_pinv.shape[0] // 3)
    width = min(16, leaves)
    leaf_major = jnp.transpose(extended.reshape(6, 3 * leaves, TILE), (1, 0, 2))
    owned_tiles = owned.reshape(6, leaves, TILE)
    gathered = jnp.take(leaf_major, neighbours[0].T - first, axis=0)
    picked = jnp.transpose(gathered, (2, 0, 1, 3)).reshape(6, leaves, -1)
    near = by_blocks(stokes_sum, [owned_tiles[:3], picked[:3], picked[3:]], leaves, width)
    centers = leaf_center[:, 0]
    multipole = moments(owned_tiles, centers, sphere, up_pinv, width)
    multipole_ext = extended_2(multipole, (("gx", 1),), leaves)
    local = leaf_translate(multipole_ext, inter_leaf[0] - first, inter_op[0], trans_ops)
    box_moment = children(multipole, child_ops)
    op_row = coarse_op[0]
    grouped = coarse_terms(op_row, lax.all_gather(box_moment, ("gx", "gy"), axis=0, tiled=True))
    local = local + downward(translate(trans_ops, grouped), child_ops, leaves)
    far = evaluate(owned_tiles, centers, sphere, local, width)
    flow = ((near + far) / (8.0 * math.pi)).reshape(3, slots)
    returning = place_rows(flow, tile_src[0], owners * capacity)
    came_back = lax.all_to_all(
        returning.reshape(3, owners, capacity), "gx", split_axis=1, concat_axis=1, tiled=True
    ).reshape(3, owners * capacity)
    return jnp.take(came_back.T, point_dest[0], axis=0).T.reshape(3, 1, count)


def solution(mesh):
    in_specs = (
        P(None, "gy", "gx"),
        P(None, "gy", "gx"),
        P(),
        P(),
        P("gy", "gx"),
        P(None, "gy", "gx"),
        P("gy", "gx"),
        P("gy", None, "gx"),
        P("gy", None, "gx"),
        P("gy", None, "gx"),
        P("gy", "gx", None),
        P(),
        P(),
        P(),
    )
    out_specs = P(None, "gy", "gx")
    return jax.shard_map(body, mesh=mesh, in_specs=in_specs, out_specs=out_specs, check_vma=False)
```

profile of v0, /device:TPU:0, one launch (start us, length us, event | category | flops | bytes accessed | tf_op | source)
XLA Modules:
  0.0 949.8 jit_solution(10576299772290023980)
XLA Ops:
  13.2 28.8 %scatter_custom_fusion = f32[32769,6]{1,0:T(8,128)} fusion(s32[8704]{0:T(1024)S(1)} %get-tuple-element.357, f32[8704,6]{1,0:T(8,128)} %copy.127, f32[]{:T(128)} %constant.187.clone.1), kind=kCustom, calls=%fused_computation.115 | custom fusion | bytes 786968 | tf_op jit(solution)/shard_map/scatter | solution.py:122
  42.0 11.2 %slice.212 = f32[32768,6]{1,0:T(8,128)} slice(f32[32769,6]{1,0:T(8,128)} %scatter_custom_fusion), slice={[0:32768], [0:6]} | slice | bytes 1572864 | tf_op jit(solution)/shard_map/slice | solution.py:123
  53.3 10.9 %copy.128 = f32[6,16,2048]{2,0,1:T(8,128)} copy(f32[6,16,2048]{0,2,1:T(8,128)} %bitcast.241) | data formatting | bytes 1572864 | tf_op jit(solution)/shard_map/reshape | solution.py:158
  64.1 8.6 all-to-all-start
  75.7 21.5 %all-to-all-done = f32[6,16,2048]{2,0,1:T(8,128)} async-done(((f32[6,16,2048]{2,0,1:T(8,128)}), f32[6,16,2048]{2,0,1:T(8,128)}, u32[]{:S(2)}, u32[]{:S(2)}) %all-to-all-start) | async-done | bytes 786464 | tf_op jit(solution)/shard_map/all_to_all | solution.py:160
  97.2 9.9 %copy.129 = f32[6,16,2048]{0,2,1:T(8,128)} copy(f32[6,16,2048]{2,0,1:T(8,128)} %all-to-all-done) | data formatting | bytes 1572864 | tf_op jit(solution)/shard_map/all_to_all | solution.py:160
  107.1 13.3 %concatenate.17 = f32[32769,6]{1,0:T(8,128)} pad(f32[32768,6]{1,0:T(8,128)} %bitcast.240, f32[]{:T(128)} %constant.187.clone.1), padding=0_1x0_0 | pad | bytes 1572892 | tf_op jit(solution)/shard_map/concatenate | solution.py:117
  120.4 114.7 %gather_fusion = f32[32768,6]{1,0:T(8,128)} fusion(f32[32769,6]{1,0:T(8,128)} %concatenate.17, s32[32768]{0:T(1024)S(1)} %broadcast_clamp_fusion), kind=kCustom, calls=%fused_computation | custom fusion | bytes 1703936 | tf_op jit(solution)/shard_map/jit(_take)/gather | solution.py:118
  235.2 17.9 %select_bitcast_fusion = f32[6,32768]{0,1:T(8,128)S(1)} fusion(f32[32768,6]{1,0:T(8,128)} %gather_fusion, pred[32768]{0:T(1024)(128)(4,1)S(1)} %compare_and_fusion), kind=kLoop, calls=%fused_computation.114 | loop fusion | flops 196608 | bytes 1605632 | tf_op jit(solution)/shard_map/jit(_take)/select_n | solution.py:118
  253.1 13.2 %fusion.71 = (f32[3,32768]{0,1:T(8,128)}, f32[3,32768]{0,1:T(8,128)}) fusion(f32[6,32768]{0,1:T(8,128)S(1)} %select_bitcast_fusion), kind=kLoop, calls=%fused_computation.178 | loop fusion | bytes 1572864 | tf_op jit(solution)/shard_map/slice | solution.py:73
  268.8 9.7 %copy.138 = f32[3,256,128]{2,1,0:T(8,128)S(1)} copy(f32[3,256,128]{0,2,1:T(8,128)} %bitcast.244) | data formatting | bytes 786432 | tf_op jit(solution)/shard_map/while | solution.py:66
  278.5 10.4 %copy.141 = f32[3,256,128]{2,1,0:T(8,128)} copy(f32[3,256,128]{0,2,1:T(8,128)} %bitcast.243) | data formatting | bytes 786432 | tf_op jit(solution)/shard_map/while | solution.py:66
  288.9 79.0 %while.37 = (s32[]{:T(128)}, f32[16,3,16,56]{3,2,1,0:T(8,128)}, s32[16]{0:T(128)S(1)}, f32[3,256,128]{2,1,0:T(8,128)}, f32[3,256,56]{2,1,0:T(8,128)S(1)}, /*inde...) while((s32[]{:T(128)}, f32[16,3,16,56]{3,2,1,0:T(8,128)}, ...), condition=%wide.region_11.12_spmd, body=%wide.region_7.11_spmd.sunk | while | flops 3558023 | bytes 226507 | solution.py:66
  376.4 10.0 %copy.130 = f32[6,32768]{1,0:T(8,128)} copy(f32[6,32768]{0,1:T(8,128)} %copy-done.1) | data formatting | bytes 1572864 | tf_op jit(solution)/shard_map/jit(_take)/select_n | solution.py:118
  386.4 5.9 collective-permute-start
  395.9 75.3 %all-reduce.1 = f32[5376]{0:T(1024)S(1)} all-reduce(f32[5376]{0:T(1024)S(1)} %dynamic-update-slice), channel_id=2, replica_groups=mesh['gx'=16,'gy'=2] {'gx','gy'}, use_global_device_ids=true, to_apply=%add.1 | all-reduce | flops 5376 | bytes 43008
  478.0 8.9 gather_fusion.2
  487.0 5.1 convolution_bitcast_fusion
  492.1 8.1 fusion.60
  500.4 80.5 %while.38 = (s32[]{:T(128)}, f32[16,3,16,128]{3,2,1,0:T(8,128)S(1)}, s32[16]{0:T(128)S(1)}, f32[3,256,56]{2,1,0:T(8,128)S(1)}, f32[3,256,128]{2,1,0:T(8,128)}, /...) while((s32[]{:T(128)}, f32[16,3,16,128]{3,2,1,0:T(8,128)S(1)}, ...), condition=%wide.region_17.18_spmd, body=%wide.region_13.17_spmd.sunk | while | flops 3561479 | bytes 212175 | solution.py:66
  580.9 3.8 maximum_bitcast_fusion.3
  584.7 4.8 gather_fusion.1
  605.5 163.1 %while.36 = (s32[]{:T(128)}, f32[16,3,16,128]{3,2,1,0:T(8,128)S(1)}, s32[16]{0:T(128)S(1)}, f32[3,256,384]{2,1,0:T(8,128)}, f32[3,256,128]{2,1,0:T(8,128)}, /*in...) while((s32[]{:T(128)}, f32[16,3,16,128]{3,2,1,0:T(8,128)S(1)}, ...), condition=%wide.region_6.7_spmd, body=%wide.region_2.6_spmd.sunk | while | flops 24385544 | bytes 590031 | solution.py:66
  609.6 6.0 fusion.93
  619.8 6.0 fusion.93
  630.0 6.0 fusion.93
  640.2 6.0 fusion.93
  650.4 6.0 fusion.93
  660.6 6.0 fusion.93
  670.8 6.0 fusion.93
  681.0 6.0 fusion.93
  691.2 6.0 fusion.93
  701.4 6.0 fusion.93
  711.6 6.0 fusion.93
  721.8 6.0 fusion.93
  732.0 6.0 fusion.93
  742.2 6.0 fusion.93
  752.4 6.0 fusion.93
  762.6 6.0 fusion.93
  769.0 8.6 copy.154
  777.6 87.1 %scatter_custom_fusion.1 = f32[32769,3]{1,0:T(8,128)} fusion(s32[32768]{0:T(1024)} %bitcast.258, f32[32768,3]{1,0:T(8,128)} %copy.154, f32[]{:T(128)} %constant.187.clone.1), kind=kCustom, calls=%fused_computation.117 | custom fusion | bytes 393740 | tf_op jit(solution)/shard_map/scatter | solution.py:122
  864.7 11.2 %slice.217 = f32[32768,3]{1,0:T(8,128)} slice(f32[32769,3]{1,0:T(8,128)} %scatter_custom_fusion.1), slice={[0:32768], [0:3]} | slice | bytes 786432 | tf_op jit(solution)/shard_map/slice | solution.py:123
  876.0 10.7 %copy.155 = f32[3,16,2048]{2,0,1:T(4,128)} copy(f32[3,16,2048]{0,2,1:T(8,128)} %bitcast.242) | data formatting | bytes 786432 | tf_op jit(solution)/shard_map/reshape | solution.py:182
  886.6 5.9 all-to-all-start.1
  892.7 14.3 %all-to-all-done.1 = f32[3,16,2048]{2,0,1:T(4,128)S(1)} async-done(((f32[3,16,2048]{2,0,1:T(4,128)}), f32[3,16,2048]{2,0,1:T(4,128)S(1)}, u32[]{:S(2)}, u32[]{:S(2)}) %all-to-all-start.1) | async-done | bytes 393248 | tf_op jit(solution)/shard_map/all_to_all | solution.py:181
  907.0 8.6 copy.156
  915.6 22.5 %gather_fusion.3 = f32[8704,3]{1,0:T(8,128)} fusion(f32[32768,3]{1,0:T(8,128)} %bitcast.239, s32[9216]{0:T(1024)S(1)} %pad_clamp_fusion), kind=kCustom, calls=%fused_computation.3 | custom fusion | bytes 243712 | tf_op jit(solution)/shard_map/jit(_take)/gather | solution.py:184
  938.1 7.8 select_bitcast_fusion.1
  (334 shorter events, 193.1 us)
Async XLA Ops:
  0.0 471.5 %copy-start = (f32[16,168,168]{2,1,0:T(8,128)S(1)}, f32[16,168,168]{2,1,0:T(8,128)}, u32[]{:S(2)}) copy-start(f32[16,168,168]{2,1,0:T(8,128)} %param.32) | copy-start | bytes 5419012
  53.2 20.0 %copy-start.14 = (s32[1,3,256]{2,0,1:T(1,128)S(1)}, s32[1,3,256]{2,0,1:T(1,128)}, u32[]{:S(2)}) copy-start(s32[1,3,256]{2,0,1:T(1,128)} %param.27) | copy-start | bytes 9220
  53.2 20.1 %copy-start.6 = (s32[1,32768]{1,0:T(1,128)S(1)}, s32[1,32768]{1,0:T(1,128)}, u32[]{:S(2)}) copy-start(s32[1,32768]{1,0:T(1,128)} %param.26) | copy-start | bytes 393220
  53.2 20.2 %copy-start.13 = (f32[3,1,256]{2,1,0:T(1,128)S(1)}, f32[3,1,256]{2,1,0:T(1,128)}, u32[]{:S(2)}) copy-start(f32[3,1,256]{2,1,0:T(1,128)} %param.25) | copy-start | bytes 9220
  53.3 20.2 %copy-start.12 = (s32[1,8,256]{2,1,0:T(8,128)S(1)}, s32[1,8,256]{2,1,0:T(8,128)}, u32[]{:S(2)}) copy-start(s32[1,8,256]{2,1,0:T(8,128)} %param.28) | copy-start | bytes 24580
  53.3 20.3 %copy-start.11 = (s32[1,8,256]{2,1,0:T(8,128)S(1)}, s32[1,8,256]{2,1,0:T(8,128)}, u32[]{:S(2)}) copy-start(s32[1,8,256]{2,1,0:T(8,128)} %param.29) | copy-start | bytes 24580
  64.1 33.1 %all-to-all-start = ((f32[6,16,2048]{2,0,1:T(8,128)}), f32[6,16,2048]{2,0,1:T(8,128)}, u32[]{:S(2)}, u32[]{:S(2)}) async-start(f32[6,16,2048]{2,0,1:T(8,128)} %copy.128), calls=%async_computation | async-start | bytes 2097152 | tf_op jit(solution)/shard_map/all_to_all | solution.py:160
  73.5 33.6 %copy-start.7 = (s32[32768,1]{0,1:T(1,128)}, s32[32768,1]{0,1:T(1,128)S(1)}, u32[]{:S(2)}) copy-start(s32[32768,1]{0,1:T(1,128)S(1)} %compare_select_fusion) | copy-start | bytes 393220
  253.1 15.7 %copy-start.1 = (f32[6,32768]{0,1:T(8,128)}, f32[6,32768]{0,1:T(8,128)S(1)}, u32[]{:S(2)}) copy-start(f32[6,32768]{0,1:T(8,128)S(1)} %select_bitcast_fusion) | copy-start | bytes 2359300
  278.5 10.4 %copy-start.16 = (s32[16]{0:T(128)S(1)}, s32[16]{0:T(128)}, u32[]{:S(2)}) copy-start(s32[16]{0:T(128)} %iota_multiply_fusion) | copy-start | bytes 196
  367.9 0.7 copy-start.3
  367.9 7.1 copy-start.4
  372.0 102.9 %collective-permute-start.2 = (f32[168,256]{1,0:T(8,128)S(1)}, f32[168,256]{1,0:T(8,128)}, u32[]{:S(2)}, u32[]{:S(2)}) collective-permute-start(f32[168,256]{1,0:T(8,128)S(1)} %convolution_bitcast_fusion.1), channel_id=1, source_target_pairs={{0,2},{2,4},{4,6},{6,8},{8,10},{10,12},{12,14},{14,16},{16,18},{18... | collective-permute-start | bytes 516104 | tf_op jit(solution)/shard_map/ppermute | solution.py:26
  375.0 99.9 %collective-permute-start.3 = (f32[168,256]{1,0:T(8,128)S(1)}, f32[168,256]{1,0:T(8,128)}, u32[]{:S(2)}, u32[]{:S(2)}) collective-permute-start(f32[168,256]{1,0:T(8,128)S(1)} %convolution_bitcast_fusion.1), channel_id=1, source_target_pairs={{2,0},{4,2},{6,4},{8,6},{10,8},{12,10},{14,12},{16,14},{18,16},{20... | collective-permute-start | bytes 516104 | tf_op jit(solution)/shard_map/ppermute | solution.py:27
  376.4 94.8 %copy-start.15 = (s32[1,1,32]{2,1,0:T(1,128)S(1)}, s32[1,1,32]{2,1,0:T(1,128)}, u32[]{:S(2)}) copy-start(s32[1,1,32]{2,1,0:T(1,128)} %param.30) | copy-start | bytes 388
  386.4 194.5 %collective-permute-start = (f32[6,32768]{1,0:T(8,128)}, f32[6,32768]{1,0:T(8,128)}, u32[]{:S(2)}, u32[]{:S(2)}) collective-permute-start(f32[6,32768]{1,0:T(8,128)} %copy.130), channel_id=1, source_target_pairs={{0,2},{2,4},{4,6},{6,8},{8,10},{10,12},{12,14},{14,16},{16,18},{18... | collective-permute-start | bytes 2359304 | tf_op jit(solution)/shard_map/ppermute | solution.py:26
  392.3 188.6 %collective-permute-start.1 = (f32[6,32768]{1,0:T(8,128)}, f32[6,32768]{1,0:T(8,128)}, u32[]{:S(2)}, u32[]{:S(2)}) collective-permute-start(f32[6,32768]{1,0:T(8,128)} %copy.130), channel_id=1, source_target_pairs={{2,0},{4,2},{6,4},{8,6},{10,8},{12,10},{14,12},{16,14},{18,16},{20... | collective-permute-start | bytes 2359304 | tf_op jit(solution)/shard_map/ppermute | solution.py:27
  471.3 1.6 copy-start.2
  487.0 5.1 copy-start.5
  584.7 4.8 copy-start.10
  876.0 16.6 %copy-start.9 = (s32[1,8704]{1,0:T(1,128)S(1)}, s32[1,8704]{1,0:T(1,128)}, u32[]{:S(2)}) copy-start(s32[1,8704]{1,0:T(1,128)} %param.24) | copy-start | bytes 104452
  876.0 16.7 %copy-start.8 = (s32[8704]{0:T(1024)S(1)}, s32[8704]{0:T(1024)}, u32[]{:S(2)}) copy-start(s32[8704]{0:T(1024)} %get-tuple-element.356) | copy-start | bytes 104452
  886.6 20.3 %all-to-all-start.1 = ((f32[3,16,2048]{2,0,1:T(4,128)}), f32[3,16,2048]{2,0,1:T(4,128)S(1)}, u32[]{:S(2)}, u32[]{:S(2)}) async-start(f32[3,16,2048]{2,0,1:T(4,128)} %copy.155), calls=%async_computation.1 | async-start | bytes 1048576 | tf_op jit(solution)/shard_map/all_to_all | solution.py:181
where the time goes:
time: 967 us; the launch traced here: 950 us
  local copies, waits for them, and re-layouts  517 us (53%)
  other arithmetic  180 us (19%)
  loops' own time  90.5 us (9%)
  blocking collectives  75.3 us (8%)
  waiting for transfers between devices  35.8 us (4%)
  starting transfers between devices  25.9 us (3%)
  matrix products  24 us (2%)
    reduce_sum x48, other arithmetic, stokes_sum(): jnp.sum(push_x * direct + projected * delta_x, axis=2)  130 us
    scatter x2, local copies, waits for them, and re-layouts, place_rows(): jnp.zeros((length + 1, values.shape[0]), jnp.float32).at[where]  116 us
    gather x1, local copies, waits for them, and re-layouts, pick_slots(): return jnp.take(rows_view, table, axis=0).T  115 us
    another operation x3, loops' own time, by_blocks(): result = lax.map(one_block, starts)  90.5 us
    unnamed x1, blocking collectives  75.3 us
    mul x48, local copies, waits for them, and re-layouts, stokes_sum(): push_y * delta_y  38.6 us
    dynamic_slice x48, local copies, waits for them, and re-layouts, by_blocks(): result = lax.map(one_block, starts)  29 us
    while x4, local copies, waits for them, and re-layouts, by_blocks(): result = lax.map(one_block, starts)  25.4 us
  transfers between devices with their start and end apart: 6, of which 2 were waited for; matrix products, arithmetic and copies ran while one was open for 10% of the time, Pallas kernels for 0%

commit v1 on v0

v1 whole, which is shorter than its diff:
```python
import functools
import math

import jax
import jax.numpy as jnp
from jax import lax
from jax.experimental import pallas as pl
from jax.experimental.pallas import tpu as pltpu
from jax.sharding import PartitionSpec as P

P_SIZE = 544
NOPS = 16
TILE = 128
L_DEV = 256


SOFTENING = 0.25
RADIUS = 2.5
HIGHEST = lax.Precision.HIGHEST


def extended_2(shard, sides, width):
    for axis, dim in sides:
        devices, length = (lax.axis_size(axis), shard.shape[dim])
        up = [(i, (i + 1) % devices) for i in range(devices - 1)]
        down = [(j, i) for i, j in up]
        last = lax.slice_in_dim(shard, length - width, length, axis=dim)
        first = lax.slice_in_dim(shard, 0, width, axis=dim)
        before = lax.ppermute(last, axis, up)
        after = lax.ppermute(first, axis, down)
        shard = jnp.concatenate([before, shard, after], axis=dim)
    return shard


def sphere_points(count):
    index = jnp.arange(count).astype(jnp.float32)
    height = 1.0 - (2.0 * index + 1.0) / count
    radial = jnp.sqrt(1.0 - height * height)
    angle = 2.399963 * index
    return jnp.stack([radial * jnp.cos(angle), radial * jnp.sin(angle), height])


LANES = 128
ROWS = 8
F32 = jnp.float32
BF16 = jnp.bfloat16
PARAMS = pltpu.CompilerParams(vmem_limit_bytes=48 * 1024 * 1024)


def split_two(value):
    high = value.astype(BF16)
    return high, (value - high.astype(F32)).astype(BF16)


def split_three(value):
    high = value.astype(BF16).astype(F32)
    rest = value - high
    middle = rest.astype(BF16).astype(F32)
    return high, middle, rest - middle


def relative(tile, center):
    row = lax.broadcasted_iota(jnp.int32, tile.shape, 0)
    shift = jnp.where(row == 0, center[0], jnp.where(row == 1, center[1], center[2]))
    return jnp.where(row < 3, tile - shift, 0.0)


def target_rows(pos):
    row = lax.broadcasted_iota(jnp.int32, pos.shape, 0)
    norm = jnp.sum(pos * pos, axis=0, keepdims=True)
    one, two, three = split_three(jnp.where(row == 3, norm, jnp.where(row == 4, 1.0, pos)))
    return jnp.concatenate([one, one, one, two, two, three], axis=0).astype(BF16)


def source_rows(pos):
    row = lax.broadcasted_iota(jnp.int32, pos.shape, 0)
    norm = jnp.sum(pos * pos, axis=0, keepdims=True) + SOFTENING
    one, two, three = split_three(jnp.where(row == 3, 1.0, jnp.where(row == 4, norm, -2.0 * pos)))
    return jnp.concatenate([one, two, three, one, two, one], axis=0).astype(BF16)


def strength_rows(pos, push):
    along = jnp.sum(push * pos[:3], axis=0, keepdims=True)
    first = jnp.concatenate([push, along, along * pos[:3], jnp.zeros_like(along)], axis=0)
    others = [push[k : k + 1] * pos for k in range(3)]
    return jnp.concatenate([first] + others, axis=0)


def pair_sum(target, source, push):
    contract = (((0,), (0,)), ((), ()))
    soft_sq = lax.dot_general(
        source_rows(source), target_rows(target), contract, preferred_element_type=F32
    )
    root = lax.rsqrt(soft_sq)
    inv_high, inv_low = split_two(root * root * root)
    root_high, root_low = split_two(root)
    high, low = split_two(strength_rows(source, push))
    both = jnp.concatenate([high, low], axis=0)
    top = jnp.concatenate([high[:16], low[:16]], axis=0)
    cubed = jnp.dot(both, inv_high, preferred_element_type=F32)
    cubed = cubed[:32] + cubed[32:] + jnp.dot(high, inv_low, preferred_element_type=F32)
    plain = jnp.dot(top, root_high, preferred_element_type=F32)
    plain = plain[:16] + plain[16:] + jnp.dot(high[:16], root_low, preferred_element_type=F32)
    at = target[:3]
    pushed = cubed[:3]
    total = plain[:3] + SOFTENING * pushed + cubed[4:7]
    total = total + at * (jnp.sum(at * pushed, axis=0, keepdims=True) - cubed[3:4])
    for k in range(3):
        total = total - at[k : k + 1] * cubed[8 + 8 * k : 11 + 8 * k]
    return total


def center_of(center_ref, leaf):
    return [center_ref[c, leaf] for c in range(3)]


def near_kernel(center_ref, index_ref, tiles_ref, out_ref):
    lists = index_ref.shape[0]
    for i in range(ROWS):
        leaf = pl.program_id(0) * ROWS + i
        center = center_of(center_ref, leaf)
        own = [tiles_ref[index_ref[n, leaf]] for n in range(lists)]
        points = [relative(tile, center) for tile in own]
        source = jnp.concatenate(points, axis=1)
        push = jnp.concatenate([tile[3:6] for tile in own], axis=1)
        total = pair_sum(points[0], source, push)
        for c in range(3):
            out_ref[c, i : i + 1, :] = total[c : c + 1]


def near_field(center, index, extended):
    leaves = center.shape[1]
    return pl.pallas_call(
        near_kernel,
        grid_spec=pltpu.PrefetchScalarGridSpec(
            num_scalar_prefetch=2,
            grid=(leaves // ROWS,),
            in_specs=[pl.BlockSpec(extended.shape, lambda s, *_: (0, 0, 0))],
            out_specs=pl.BlockSpec((3, ROWS, LANES), lambda s, *_: (0, s, 0)),
        ),
        out_shape=jax.ShapeDtypeStruct((3, leaves, LANES), F32),
        compiler_params=PARAMS,
        name="near_field",
    )(center, index, extended)


def check_kernel(center_ref, tiles_ref, surface_ref, out_ref):
    for i in range(ROWS):
        center = center_of(center_ref, pl.program_id(0) * ROWS + i)
        tile = tiles_ref[i]
        total = pair_sum(surface_ref[...], relative(tile, center), tile[3:6])
        for c in range(3):
            out_ref[c, i : i + 1, :] = total[c : c + 1]


def check_values(center, tiles, surface):
    leaves = center.shape[1]
    return pl.pallas_call(
        check_kernel,
        grid_spec=pltpu.PrefetchScalarGridSpec(
            num_scalar_prefetch=1,
            grid=(leaves // ROWS,),
            in_specs=[
                pl.BlockSpec((ROWS, ROWS, LANES), lambda s, *_: (s, 0, 0)),
                pl.BlockSpec((ROWS, LANES), lambda s, *_: (0, 0)),
            ],
            out_specs=pl.BlockSpec((3, ROWS, LANES), lambda s, *_: (0, s, 0)),
        ),
        out_shape=jax.ShapeDtypeStruct((3, leaves, LANES), F32),
        compiler_params=PARAMS,
        name="check_values",
    )(center, tiles, surface)


def far_kernel(center_ref, tiles_ref, surface_ref, local_ref, near_ref, out_ref):
    for i in range(ROWS):
        center = center_of(center_ref, pl.program_id(0) * ROWS + i)
        push = jnp.concatenate([local_ref[c, i : i + 1, :] for c in range(3)], axis=0)
        total = pair_sum(relative(tiles_ref[i], center), surface_ref[...], push)
        for c in range(3):
            both = near_ref[c, i : i + 1, :] + total[c : c + 1]
            out_ref[c, i : i + 1, :] = both * (1.0 / (8.0 * math.pi))


def far_field(center, tiles, surface, local, near):
    leaves = center.shape[1]
    rows_spec = pl.BlockSpec((3, ROWS, LANES), lambda s, *_: (0, s, 0))
    return pl.pallas_call(
        far_kernel,
        grid_spec=pltpu.PrefetchScalarGridSpec(
            num_scalar_prefetch=1,
            grid=(leaves // ROWS,),
            in_specs=[
                pl.BlockSpec((ROWS, ROWS, LANES), lambda s, *_: (s, 0, 0)),
                pl.BlockSpec((ROWS, LANES), lambda s, *_: (0, 0)),
                rows_spec,
                rows_spec,
            ],
            out_specs=rows_spec,
        ),
        out_shape=jax.ShapeDtypeStruct((3, leaves, LANES), F32),
        compiler_params=PARAMS,
        name="far_field",
    )(center, tiles, surface, local, near)


def scatter_kernel(where_ref, value_ref, out_ref, total_ref):
    parts, kinds, rows, _ = out_ref.shape
    where = where_ref[...]
    high_at, low_at = where >> 7, where & 127
    rows_iota = lax.broadcasted_iota(jnp.int32, (parts * rows, LANES), 0)
    lane_iota = lax.broadcasted_iota(jnp.int32, (LANES, LANES), 0)
    chosen = [rows_iota == high_at[i : i + 1] for i in range(ROWS)]
    onehot = jnp.concatenate([jnp.where(x, 1.0, 0.0).astype(BF16) for x in chosen], axis=1)
    lanes = [lane_iota == low_at[i : i + 1] for i in range(ROWS)]

    @pl.when(pl.program_id(0) == 0)
    def _():
        total_ref[...] = jnp.zeros_like(total_ref)

    for c in range(kinds):
        pieces = split_three(value_ref[c])
        spread = [
            jnp.concatenate(
                [jnp.where(lanes[i], x[i : i + 1], 0.0).astype(BF16) for i in range(ROWS)], axis=1
            )
            for x in pieces
        ]
        for pair in (spread[:2], spread[2:]):
            got = lax.dot_general(
                onehot,
                jnp.concatenate(pair, axis=0) if len(pair) > 1 else pair[0],
                (((1,), (1,)), ((), ())),
                preferred_element_type=F32,
            )
            for k in range(len(pair)):
                total_ref[c] += got[:, k * LANES : (k + 1) * LANES]

    @pl.when(pl.program_id(0) == pl.num_programs(0) - 1)
    def _():
        for part in range(parts):
            for c in range(kinds):
                out_ref[part, c] = total_ref[c, part * rows : (part + 1) * rows]


def scatter_rows(values, where, parts, rows):
    kinds, count = values.shape[:2]
    shape = (parts, kinds, rows, LANES)
    return pl.pallas_call(
        scatter_kernel,
        grid=(count // ROWS,),
        in_specs=[
            pl.BlockSpec((ROWS, LANES), lambda s: (s, 0)),
            pl.BlockSpec((kinds, ROWS, LANES), lambda s: (0, s, 0)),
        ],
        out_specs=pl.BlockSpec(shape, lambda s: (0, 0, 0, 0)),
        out_shape=jax.ShapeDtypeStruct(shape, F32),
        scratch_shapes=[pltpu.VMEM((kinds, parts * rows, LANES), F32)],
        compiler_params=PARAMS,
        name="scatter_rows",
    )(where, values)


def gather_kernel(leaf_major, where_ref, table_ref, out_ref):
    parts, kinds, rows, _ = table_ref.shape
    where = where_ref[...]
    high_at, low_at = where >> 7, where & 127

    def one_part(part, found):
        found = list(found)
        for k in range(rows):
            here = high_at == part * rows + k
            for c in range(kinds):
                line = jnp.broadcast_to(table_ref[part, c, k : k + 1, :], where.shape)
                got = jnp.take_along_axis(line, low_at, axis=1)
                found[c] = jnp.where(here, got, found[c])
        return tuple(found)

    zero = jnp.zeros(where.shape, F32)
    found = lax.fori_loop(0, parts, one_part, (zero,) * kinds)
    if leaf_major:
        for c in range(ROWS):
            out_ref[:, c, :] = found[c] if c < kinds else zero
    else:
        for c in range(kinds):
            out_ref[c] = found[c]


def gather_rows(table, where, leaf_major):
    kinds, count = table.shape[1], where.shape[0]
    if leaf_major:
        shape = (count, ROWS, LANES)
        out_spec = pl.BlockSpec((ROWS, ROWS, LANES), lambda s: (s, 0, 0))
    else:
        shape = (kinds, count, LANES)
        out_spec = pl.BlockSpec((kinds, ROWS, LANES), lambda s: (0, s, 0))
    return pl.pallas_call(
        functools.partial(gather_kernel, leaf_major),
        grid=(count // ROWS,),
        in_specs=[
            pl.BlockSpec((ROWS, LANES), lambda s: (s, 0)),
            pl.BlockSpec(table.shape, lambda s: (0, 0, 0, 0)),
        ],
        out_specs=out_spec,
        out_shape=jax.ShapeDtypeStruct(shape, F32),
        compiler_params=PARAMS,
        name="gather_rows",
    )(where, table)


def gather_boxes(own, axes):
    held = own
    for axis in reversed(axes):
        step = 1
        while step < lax.axis_size(axis):
            pairs = [(i, i ^ step) for i in range(lax.axis_size(axis))]
            other = lax.ppermute(held, axis, pairs)
            upper = (lax.axis_index(axis) // step) % 2 == 1
            held = jnp.where(
                upper,
                jnp.concatenate([other, held], axis=0),
                jnp.concatenate([held, other], axis=0),
            )
            step *= 2
    return held


def pad_rows(array, count, fill):
    wide = ROWS * LANES
    total = -(-count // wide) * wide
    pad = [(0, 0)] * (array.ndim - 1) + [(0, total - count)]
    padded = jnp.pad(array, pad, constant_values=fill)
    return padded.reshape(array.shape[:-1] + (total // LANES, LANES))


def children(multipole, child_ops):
    expansion = multipole.shape[0]
    grouped = jnp.sum(multipole.reshape(expansion, -1, L_DEV // 8, 8), axis=2)
    return jnp.einsum("cef,ebc->bf", child_ops, grouped, precision=HIGHEST)


def coarse_terms(op_rows, coarse):
    onehot = (op_rows[:, :, None] == jnp.arange(NOPS)[None, None, :]).astype(jnp.float32)
    return jnp.einsum("tbk,be->tke", onehot, coarse, precision=HIGHEST)


def translate(trans_ops, grouped):
    return jnp.einsum("kef,tke->tf", trans_ops, grouped, precision=HIGHEST)


def leaf_translate(extended, index, op_rows, trans_ops):
    picked = extended[:, index]
    onehot = (op_rows[:, :, None] == jnp.arange(NOPS)[None, None, :]).astype(jnp.float32)
    grouped = jnp.einsum("ejn,jnk->ken", picked, onehot, precision=HIGHEST)
    return jnp.einsum("kef,ken->fn", trans_ops, grouped, precision=HIGHEST)


def downward(coarse_local, child_ops, leaves):
    pushed = jnp.einsum("cfe,be->fbc", child_ops, coarse_local, precision=HIGHEST)
    expansion = pushed.shape[0]
    boxes = pushed.shape[1]
    spread = jnp.broadcast_to(pushed[:, :, None, :], (expansion, boxes, leaves // 8, 8))
    return spread.reshape(expansion, boxes * leaves)


def body(
    positions,
    forces,
    deriv_mat,
    quad_mat,
    point_dest,
    leaf_center,
    tile_src,
    neighbours,
    inter_leaf,
    inter_op,
    coarse_op,
    up_pinv,
    trans_ops,
    child_ops,
):
    owners = lax.axis_size("gx")
    count = positions.shape[2]
    leaves = leaf_center.shape[2]
    slots = leaves * TILE
    capacity = slots // owners
    tangent = jnp.dot(
        positions.reshape(-1, P_SIZE),
        deriv_mat,
        precision=HIGHEST,
        preferred_element_type=jnp.float32,
    ).reshape(3, count)
    jacobian = jnp.sqrt(1.0 + jnp.sum(tangent * tangent, axis=0))
    weighted = jnp.dot(
        forces.reshape(-1, P_SIZE), quad_mat, precision=HIGHEST, preferred_element_type=jnp.float32
    ).reshape(3, count)
    packed = jnp.concatenate([positions.reshape(3, count), weighted * jacobian[None]], axis=0)
    rows = capacity // LANES
    outgoing = scatter_rows(
        pad_rows(packed, count, 0.0), pad_rows(point_dest[0], count, -1), owners, rows
    )
    first = lax.axis_index("gx") * leaves - leaves
    arrived = lax.all_to_all(outgoing, "gx", split_axis=0, concat_axis=0, tiled=True)
    table = tile_src[0].reshape(leaves, TILE)
    tiles = gather_rows(arrived, table, True)
    extended = extended_2(tiles, (("gx", 0),), leaves)
    points = up_pinv.shape[0] // 3
    surface = jnp.pad(RADIUS * sphere_points(points), ((0, ROWS - 3), (0, LANES - points)))
    centers = leaf_center[:, 0]
    checks = check_values(centers, tiles, surface)[:, :, :points]
    stacked = jnp.transpose(checks, (0, 2, 1)).reshape(3 * points, leaves)
    multipole = jnp.dot(up_pinv.T, stacked, precision=HIGHEST, preferred_element_type=F32)
    multipole_ext = extended_2(multipole, (("gx", 1),), leaves)
    gathered = gather_boxes(children(multipole, child_ops), ("gx", "gy"))
    near = near_field(centers, neighbours[0] - first, extended)
    local = leaf_translate(multipole_ext, inter_leaf[0] - first, inter_op[0], trans_ops)
    grouped = coarse_terms(coarse_op[0], gathered)
    local = local + downward(translate(trans_ops, grouped), child_ops, leaves)
    density = jnp.transpose(local.reshape(3, points, leaves), (0, 2, 1))
    density = jnp.pad(density, ((0, 0), (0, 0), (0, LANES - points)))
    flow = far_field(centers, tiles, surface, density, near)
    returning = scatter_rows(flow, table, owners, rows)
    came_back = lax.all_to_all(returning, "gx", split_axis=0, concat_axis=0, tiled=True)
    found = gather_rows(came_back, pad_rows(point_dest[0], count, 0), False)
    return found.reshape(3, -1)[:, :count].reshape(3, 1, count)


def solution(mesh):
    in_specs = (
        P(None, "gy", "gx"),
        P(None, "gy", "gx"),
        P(),
        P(),
        P("gy", "gx"),
        P(None, "gy", "gx"),
        P("gy", "gx"),
        P("gy", None, "gx"),
        P("gy", None, "gx"),
        P("gy", None, "gx"),
        P("gy", "gx", None),
        P(),
        P(),
        P(),
    )
    out_specs = P(None, "gy", "gx")
    return jax.shard_map(body, mesh=mesh, in_specs=in_specs, out_specs=out_specs, check_vma=False)
```

time: 967 us -> 466 us (0.48); the launches traced: 950 us -> 465 us
  local copies, waits for them, and re-layouts: 517 us -> 17.8 us
  Pallas kernels: 0 us -> 332 us
  other arithmetic: 180 us -> 7.18 us
  loops' own time: 90.5 us -> 0 us
  blocking collectives: 75.3 us -> 14.7 us
    pallas_call x0 -> x7, Pallas kernels: none -> 332 us  [the longest x2 106 us: gather_rows(): pl.pallas_call(functools.partial(gather_kernel, leaf_major), grid=(count...]
    gather x3 -> x0, local copies, waits for them, and re-layouts: 142 us -> none  [the longest x1 115 us: pick_slots(): return jnp.take(rows_view, table, axis=0).T]
    reduce_sum x48 -> x0, other arithmetic: 130 us -> none  [stokes_sum(): jnp.sum(push_x * direct + projected * delta_x, axis=2)]
    scatter x2 -> x0, local copies, waits for them, and re-layouts: 116 us -> none  [place_rows(): jnp.zeros((length + 1, values.shape[0]), jnp.float32).at[where]]
    another operation x3 -> x0, loops' own time: 90.5 us -> none  [by_blocks(): result = lax.map(one_block, starts)]
    unnamed x1 -> x0, blocking collectives: 75.3 us -> none
    slice x6 -> x1, local copies, waits for them, and re-layouts: 42.8 us -> 0.03 us  [body(): return found.reshape(3, -1)[:, :count].reshape(3, 1, count)]
    mul x48 -> x0, local copies, waits for them, and re-layouts: 38.6 us -> none  [stokes_sum(): push_y * delta_y]
  transfers between devices with their start and end apart: 6 -> 10, of which waited for: 2 -> 6; matrix products, arithmetic and copies ran while one was open for 10% -> 6% of each run, Pallas kernels for 0% -> 0%
where the time goes in v1:
time: 466 us; the launch traced here: 465 us
  Pallas kernels  332 us (71%)
  waiting for transfers between devices  42.1 us (9%)
  starting transfers between devices  27.6 us (6%)
  matrix products  23 us (5%)
  local copies, waits for them, and re-layouts  17.8 us (4%)
  blocking collectives  14.7 us (3%)
  other arithmetic  7.18 us (2%)
    pallas_call x2, Pallas kernels, gather_rows(): pl.pallas_call(functools.partial(gather_kernel, leaf_major), grid=(count...  106 us
    pallas_call x1, Pallas kernels, near_field(): pl.pallas_call(near_kernel, grid_spec=pltpu.PrefetchScalarGridSpec(num_sc...  69.6 us
    pallas_call x2, Pallas kernels, scatter_rows(): pl.pallas_call(scatter_kernel, grid=(count // ROWS,), in_specs=[pl.BlockS...  58 us
    pallas_call x1, Pallas kernels, far_field(): pl.pallas_call(far_kernel, grid_spec=pltpu.PrefetchScalarGridSpec(num_sca...  49.3 us
    pallas_call x1, Pallas kernels, check_values(): pl.pallas_call(check_kernel, grid_spec=pltpu.PrefetchScalarGridSpec(num_s...  49.2 us
    all_to_all x1, waiting for transfers between devices, body(): lax.all_to_all(outgoing, 'gx', split_axis=0, concat_axis=0, tiled=True)  19.6 us
    ppermute x2, waiting for transfers between devices, extended_2(): before = lax.ppermute(last, axis, up)  15.3 us
    all_to_all x1, blocking collectives, body(): lax.all_to_all(returning, 'gx', split_axis=0, concat_axis=0, tiled=True)  14.7 us
  transfers between devices with their start and end apart: 10, of which 6 were waited for; matrix products, arithmetic and copies ran while one was open for 6% of the time, Pallas kernels for 0%

profile of v1, /device:TPU:0, one launch (start us, length us, event | category | flops | bytes accessed | tf_op | source)
XLA Modules:
  0.0 464.9 jit_solution(8989213180393359952)
XLA Ops:
  0.0 1.0 reduce.1
  1.0 0.6 pad_bitcast_fusion
  1.6 0.9 copy.68
  2.6 1.2 reduce.3
  3.7 1.2 reduce.2
  5.1 2.3 fusion.24
  7.6 2.3 convolution_multiply_fusion
  10.3 19.3 %scatter_rows.2 = f32[16,6,16,128]{3,2,1,0:T(8,128)} custom-call(s32[72,128]{1,0:T(8,128)S(1)} %get-tuple-element.5.where_ref, f32[6,72,128]{2,1,0:T(8,128)S(1)} %bitcast.81), custom_call_target="tpu_custom_call" | custom-call | tf_op jit(solution)/shard_map/scatter_rows/pallas_call | solution.py:249
  29.6 8.3 %all-to-all-start = ((f32[16,6,16,128]{3,2,1,0:T(8,128)}), f32[16,6,16,128]{3,2,1,0:T(8,128)S(1)}, u32[]{:S(2)}, u32[]{:S(2)}) async-start(f32[16,6,16,128]{3,2,1,0:T(8,128)} %scatter_rows.2), calls=%async_computation | async-start | bytes 1572864 | tf_op jit(solution)/shard_map/all_to_all | solution.py:403
  38.1 19.6 %all-to-all-done.table_ref = f32[16,6,16,128]{3,2,1,0:T(8,128)S(1)} async-done(((f32[16,6,16,128]{3,2,1,0:T(8,128)}), f32[16,6,16,128]{3,2,1,0:T(8,128)S(1)}, u32[]{:S(2)}, u32[]{:S(2)}) %all-to-all-start) | async-done | bytes 786464 | tf_op jit(solution)/shard_map/all_to_all | solution.py:403
  57.7 0.9 copy-done.3
  58.6 88.5 %gather_rows.2.tiles_ref = f32[256,8,128]{2,1,0:T(8,128)S(1)} custom-call(s32[256,128]{1,0:T(8,128)S(1)} %bitcast.82, f32[16,6,16,128]{3,2,1,0:T(8,128)S(1)} %all-to-all-done.table_ref), custom_call_target="tpu_custom_call" | custom-call | tf_op jit(solution)/shard_map/gather_rows/pallas_call | solution.py:297
  147.1 49.2 %check_values.1 = f32[3,256,128]{2,1,0:T(8,128)S(1)} custom-call(f32[3,256]{1,0:T(4,128)S(1)} %bitcast.85, f32[256,8,128]{2,1,0:T(8,128)S(1)} %gather_rows.2.tiles_ref, f32[8,128]{1,0:T(8,128)S(1)} %pad.22.surface_ref), custom_call_target="tpu_custom_call" | custom-call | tf_op jit(solution)/shard_map/check_values/pallas_call | solution.py:158
  196.4 1.0 copy-done.1
  197.5 0.5 convolution_bitcast_fusion.1
  198.2 2.0 convolution_bitcast_fusion.4
  200.3 1.1 collective-permute-done.2
  201.4 0.6 collective-permute-start.3
  202.1 3.0 collective-permute-done.3
  205.1 1.7 collective-permute-start.4
  206.8 2.0 collective-permute-done.4
  208.8 2.2 collective-permute-start.5
  211.0 0.6 broadcast_clamp_fusion
  211.6 1.0 collective-permute-done.5
  212.6 1.6 collective-permute-start.6
  214.2 0.8 copy.25
  215.0 1.4 collective-permute-start.1
  216.4 4.6 collective-permute-start
  221.0 1.3 collective-permute-start.8
  222.3 5.9 %collective-permute-start.7 = (f32[256,8,128]{2,1,0:T(8,128)}, f32[256,8,128]{2,1,0:T(8,128)}, u32[]{:S(2)}, u32[]{:S(2)}) collective-permute-start(f32[256,8,128]{2,1,0:T(8,128)} %copy-done.1), channel_id=1, source_target_pairs={{0,2},{2,4},{4,6},{6,8},{8,10},{10,12},{12,14},{14,16},{16,18},{18... | collective-permute-start | bytes 3145736 | tf_op jit(solution)/shard_map/ppermute | solution.py:29
  228.2 0.3 convolution_bitcast_fusion.2
  228.5 1.3 convolution_bitcast_fusion.3
  229.7 1.2 fusion.25
  231.0 0.8 copy.32
  231.8 15.3 %collective-permute-done = f32[168,256]{1,0:T(8,128)S(1)} collective-permute-done((f32[168,256]{1,0:T(8,128)S(1)}, f32[168,256]{1,0:T(8,128)S(1)}, u32[]{:S(2)}, u32[]{:S(2)}) %collective-permute-start) | collective-permute-done | bytes 172064 | tf_op jit(solution)/shard_map/ppermute | solution.py:29
  247.1 0.8 pad_maximum_fusion.1
  247.9 1.3 copy.27
  249.2 9.5 %gather_fusion = f32[2048,168]{1,0:T(8,128)} fusion(f32[168,768]{0,1:T(8,128)S(1)} %copy.27, s32[2048]{0:T(1024)} %broadcast_clamp_fusion), kind=kCustom, calls=%fused_computation | custom fusion | bytes 2760704 | tf_op jit(solution)/shard_map/gather | solution.py:352
  258.7 5.0 %convolution_bitcast_fusion = f32[16,168,256]{1,0,2:T(8,128)S(1)} fusion(f32[8,256,168]{2,1,0:T(8,128)} %bitcast.88, s32[8,256]{0,1:T(8,128)} %copy.25), kind=kOutput, calls=%fused_computation.4 | convolution fusion | flops 66093056 | bytes 4136960 | tf_op jit(solution)/shard_map/ejn,jnk->ken/dot_general | solution.py:354
  263.8 8.1 %fusion.7 = f32[168,256]{1,0:T(8,128)S(1)} fusion(f32[168,256]{1,0:T(8,128)S(1)} %copy-done.7, f32[16,168,168]{2,1,0:T(8,128)S(1)} %copy-done, f32[16,168,256]{1,0,2:T(8,128)S(1)} %convolution_bitcast_fusion), kind=kOutput, calls=%fused_computation.10 | convolution fusion | flops 1387309056 | bytes 4902912 | tf_op jit(solution)/shard_map/kef,ken->fn/dot_general | solution.py:355
  271.9 0.2 copy.33
  272.1 2.1 pad_maximum_fusion.tiles_ref
  274.2 69.6 %near_field.1.near_ref = f32[3,256,128]{2,1,0:T(8,128)S(1)} custom-call(f32[3,256]{1,0:T(4,128)S(1)} %bitcast.86, s32[3,256]{1,0:T(4,128)S(1)} %fusion.22.index_ref, f32[768,8,128]{2,1,0:T(8,128)S(1)} %pad_maximum_fusion.tiles_ref), custom_call_target="tpu_custom_call" | custom-call | tf_op jit(solution)/shard_map/near_field/pallas_call | solution.py:133
  343.9 49.3 %far_field.1.value_ref = f32[3,256,128]{2,1,0:T(8,128)S(1)} custom-call(f32[3,256]{1,0:T(4,128)S(1)} %bitcast.87, f32[256,8,128]{2,1,0:T(8,128)S(1)} %copy-done.2, f32[8,128]{1,0:T(8,128)S(1)} %pad.22.surface_ref, f32[3,256,128]{2,1,0:T(8,128)S(1)} %pad.23.local_ref, f32[3,256,128]{2,1,0:T(8,128)S(1)} %near_field.1.near_ref), custom_call_target="tpu_custom_call" | custom-call | tf_op jit(solution)/shard_map/far_field/pallas_call | solution.py:188
  393.2 38.8 %scatter_rows.3 = f32[16,3,16,128]{3,2,1,0:T(8,128)S(1)} custom-call(s32[256,128]{1,0:T(8,128)S(1)} %bitcast.83, f32[3,256,128]{2,1,0:T(8,128)S(1)} %far_field.1.value_ref), custom_call_target="tpu_custom_call" | custom-call | tf_op jit(solution)/shard_map/scatter_rows/pallas_call | solution.py:249
  432.0 14.7 %all_to_all.10.table_ref = f32[16,3,16,128]{3,2,1,0:T(8,128)S(1)} all-to-all(f32[16,3,16,128]{3,2,1,0:T(8,128)S(1)} %scatter_rows.3), channel_id=1, replica_groups=mesh['gx'=16,'gy'=2] {'gx'}, dimensions={0} | all-to-all | bytes 786432 | tf_op jit(solution)/shard_map/all_to_all | solution.py:423
  446.7 17.4 %gather_rows.3 = f32[3,72,128]{2,1,0:T(8,128)S(1)} custom-call(s32[72,128]{1,0:T(8,128)S(1)} %copy-done.5, f32[16,3,16,128]{3,2,1,0:T(8,128)S(1)} %all_to_all.10.table_ref), custom_call_target="tpu_custom_call" | custom-call | tf_op jit(solution)/shard_map/gather_rows/pallas_call | solution.py:297
  464.2 0.7 reshape.151
  (61 shorter events, 1.5 us)
Async XLA Ops:
  0.0 228.5 %copy-start = (f32[16,168,168]{2,1,0:T(8,128)S(1)}, f32[16,168,168]{2,1,0:T(8,128)}, u32[]{:S(2)}) copy-start(f32[16,168,168]{2,1,0:T(8,128)} %param.26) | copy-start | bytes 5419012
  10.0 27.9 %copy-start.11 = (f32[3,1,256]{2,1,0:T(1,128)S(1)}, f32[3,1,256]{2,1,0:T(1,128)}, u32[]{:S(2)}) copy-start(f32[3,1,256]{2,1,0:T(1,128)} %param.19) | copy-start | bytes 9220
  29.6 28.1 %all-to-all-start = ((f32[16,6,16,128]{3,2,1,0:T(8,128)}), f32[16,6,16,128]{3,2,1,0:T(8,128)S(1)}, u32[]{:S(2)}, u32[]{:S(2)}) async-start(f32[16,6,16,128]{3,2,1,0:T(8,128)} %scatter_rows.2), calls=%async_computation | async-start | bytes 1572864 | tf_op jit(solution)/shard_map/all_to_all | solution.py:403
  57.7 0.9 copy-start.3
  147.1 50.4 %copy-start.8 = (f32[168,168]{1,0:T(8,128)S(1)}, f32[168,168]{1,0:T(8,128)}, u32[]{:S(2)}) copy-start(f32[168,168]{1,0:T(8,128)} %param.25) | copy-start | bytes 338692
  196.4 1.0 copy-start.1
  197.3 9.4 %copy-start.10 = (s32[1,8,256]{2,1,0:T(8,128)S(1)}, s32[1,8,256]{2,1,0:T(8,128)}, u32[]{:S(2)}) copy-start(s32[1,8,256]{2,1,0:T(8,128)} %param.22) | copy-start | bytes 24580
  197.3 16.9 %copy-start.12 = (s32[1,3,256]{2,0,1:T(1,128)S(1)}, s32[1,3,256]{2,0,1:T(1,128)}, u32[]{:S(2)}) copy-start(s32[1,3,256]{2,0,1:T(1,128)} %param.21) | copy-start | bytes 9220
  197.3 16.9 %copy-start.9 = (s32[1,8,256]{2,1,0:T(8,128)S(1)}, s32[1,8,256]{2,1,0:T(8,128)}, u32[]{:S(2)}) copy-start(s32[1,8,256]{2,1,0:T(8,128)} %param.23) | copy-start | bytes 24580
  197.3 30.9 %copy-start.13 = (s32[1,1,32]{2,1,0:T(1,128)S(1)}, s32[1,1,32]{2,1,0:T(1,128)}, u32[]{:S(2)}) copy-start(s32[1,1,32]{2,1,0:T(1,128)} %param.24) | copy-start | bytes 388
  200.3 1.1 collective-permute-start.2
  201.4 3.7 collective-permute-start.3
  205.1 3.7 collective-permute-start.4
  208.8 3.8 collective-permute-start.5
  212.6 15.6 %collective-permute-start.6 = (f32[16,168]{1,0:T(8,128)S(1)}, f32[16,168]{1,0:T(8,128)S(1)}, u32[]{:S(2)}, u32[]{:S(2)}) collective-permute-start(f32[16,168]{1,0:T(8,128)S(1)} %maximum_select_fusion.2), channel_id=1, source_target_pairs={{0,16},{2,18},{4,20},{6,22},{8,24},{10,26},{12,28},{14,30},{16,0},... | collective-permute-start | bytes 32264 | tf_op jit(solution)/shard_map/ppermute | solution.py:317
  215.0 14.7 %copy-start.6 = (f32[8,168,168]{2,1,0:T(8,128)S(1)}, f32[8,168,168]{2,1,0:T(8,128)}, u32[]{:S(2)}) copy-start(f32[8,168,168]{2,1,0:T(8,128)} %param.27) | copy-start | bytes 2709508
  215.0 16.8 %collective-permute-start.1 = (f32[168,256]{1,0:T(8,128)S(1)}, f32[168,256]{1,0:T(8,128)S(1)}, u32[]{:S(2)}, u32[]{:S(2)}) collective-permute-start(f32[168,256]{1,0:T(8,128)S(1)} %convolution_bitcast_fusion.1), channel_id=1, source_target_pairs={{2,0},{4,2},{6,4},{8,6},{10,8},{12,10},{14,12},{16,14},{18,16},{20... | collective-permute-start | bytes 516104 | tf_op jit(solution)/shard_map/ppermute | solution.py:30
  216.4 30.7 %collective-permute-start = (f32[168,256]{1,0:T(8,128)S(1)}, f32[168,256]{1,0:T(8,128)S(1)}, u32[]{:S(2)}, u32[]{:S(2)}) collective-permute-start(f32[168,256]{1,0:T(8,128)S(1)} %convolution_bitcast_fusion.1), channel_id=1, source_target_pairs={{0,2},{2,4},{4,6},{6,8},{8,10},{10,12},{12,14},{14,16},{16,18},{18... | collective-permute-start | bytes 516104 | tf_op jit(solution)/shard_map/ppermute | solution.py:29
  221.0 51.1 %collective-permute-start.8 = (f32[256,8,128]{2,1,0:T(8,128)}, f32[256,8,128]{2,1,0:T(8,128)}, u32[]{:S(2)}, u32[]{:S(2)}) collective-permute-start(f32[256,8,128]{2,1,0:T(8,128)} %copy-done.1), channel_id=1, source_target_pairs={{2,0},{4,2},{6,4},{8,6},{10,8},{12,10},{14,12},{16,14},{18,16},{20... | collective-permute-start | bytes 3145736 | tf_op jit(solution)/shard_map/ppermute | solution.py:30
  222.3 49.8 %collective-permute-start.7 = (f32[256,8,128]{2,1,0:T(8,128)}, f32[256,8,128]{2,1,0:T(8,128)}, u32[]{:S(2)}, u32[]{:S(2)}) collective-permute-start(f32[256,8,128]{2,1,0:T(8,128)} %copy-done.1), channel_id=1, source_target_pairs={{0,2},{2,4},{4,6},{6,8},{8,10},{10,12},{12,14},{14,16},{16,18},{18... | collective-permute-start | bytes 3145736 | tf_op jit(solution)/shard_map/ppermute | solution.py:29
  258.7 5.1 %copy-start.7 = (f32[168,256]{1,0:T(8,128)S(1)}, f32[168,256]{1,0:T(8,128)}, u32[]{:S(2)}) copy-start(f32[168,256]{1,0:T(8,128)} %copy.32) | copy-start | bytes 516100
  274.2 69.7 %copy-start.2 = (f32[256,8,128]{2,1,0:T(8,128)S(1)}, f32[256,8,128]{2,1,0:T(8,128)}, u32[]{:S(2)}) copy-start(f32[256,8,128]{2,1,0:T(8,128)} %copy-done.1) | copy-start | bytes 3145732
  274.2 119.0 %copy-start.4 = (s32[1,32768]{1,0:T(1,128)S(1)}, s32[1,32768]{1,0:T(1,128)}, u32[]{:S(2)}) copy-start(s32[1,32768]{1,0:T(1,128)} %param.20) | copy-start | bytes 393220
  343.9 102.8 %copy-start.5 = (s32[72,128]{1,0:T(8,128)S(1)}, s32[72,128]{1,0:T(8,128)}, u32[]{:S(2)}) copy-start(s32[72,128]{1,0:T(8,128)} %get-tuple-element.6.where_ref) | copy-start | bytes 110596

commit v2 on v1

--- a/solution.py
+++ b/solution.py
@@ -92,13 +92,17 @@
         source_rows(source), target_rows(target), contract, preferred_element_type=F32
     )
     root = lax.rsqrt(soft_sq)
-    inv_high, inv_low = split_two(root * root * root)
+    inverse = [x.astype(BF16) for x in split_three(root * root * root)]
     root_high, root_low = split_two(root)
-    high, low = split_two(strength_rows(source, push))
-    both = jnp.concatenate([high, low], axis=0)
+    strength = [x.astype(BF16) for x in split_three(strength_rows(source, push))]
+    high, low = strength[:2]
+    cubed = jnp.zeros((32, target.shape[1]), F32)
+    for k in range(3):
+        both = jnp.concatenate(strength[: 3 - k], axis=0)
+        part = jnp.dot(both, inverse[k], preferred_element_type=F32)
+        for j in range(3 - k):
+            cubed = cubed + part[32 * j : 32 * j + 32]
     top = jnp.concatenate([high[:16], low[:16]], axis=0)
-    cubed = jnp.dot(both, inv_high, preferred_element_type=F32)
-    cubed = cubed[:32] + cubed[32:] + jnp.dot(high, inv_low, preferred_element_type=F32)
     plain = jnp.dot(top, root_high, preferred_element_type=F32)
     plain = plain[:16] + plain[16:] + jnp.dot(high[:16], root_low, preferred_element_type=F32)
     at = target[:3]

time: 466 us -> 466 us (level)
  no operation moved by 1% of the time
where the time goes in v2:
time: 466 us; the launch traced here: 465 us
  Pallas kernels  332 us (71%)
  waiting for transfers between devices  42.1 us (9%)
  starting transfers between devices  27.6 us (6%)
  matrix products  23 us (5%)
  local copies, waits for them, and re-layouts  17.8 us (4%)
  blocking collectives  14.7 us (3%)
  other arithmetic  7.18 us (2%)
    pallas_call x2, Pallas kernels, gather_rows(): pl.pallas_call(functools.partial(gather_kernel, leaf_major), grid=(count...  106 us
    pallas_call x1, Pallas kernels, near_field(): pl.pallas_call(near_kernel, grid_spec=pltpu.PrefetchScalarGridSpec(num_sc...  68.5 us
    pallas_call x2, Pallas kernels, scatter_rows(): pl.pallas_call(scatter_kernel, grid=(count // ROWS,), in_specs=[pl.BlockS...  58 us
    pallas_call x1, Pallas kernels, check_values(): pl.pallas_call(check_kernel, grid_spec=pltpu.PrefetchScalarGridSpec(num_s...  49.8 us
    pallas_call x1, Pallas kernels, far_field(): pl.pallas_call(far_kernel, grid_spec=pltpu.PrefetchScalarGridSpec(num_sca...  49.8 us
    all_to_all x1, waiting for transfers between devices, body(): lax.all_to_all(outgoing, 'gx', split_axis=0, concat_axis=0, tiled=True)  19.6 us
    ppermute x2, waiting for transfers between devices, extended_2(): before = lax.ppermute(last, axis, up)  15.3 us
    all_to_all x1, blocking collectives, body(): lax.all_to_all(returning, 'gx', split_axis=0, concat_axis=0, tiled=True)  14.7 us
  transfers between devices with their start and end apart: 10, of which 6 were waited for; matrix products, arithmetic and copies ran while one was open for 6% of the time, Pallas kernels for 0%

profile of v2, /device:TPU:0, one launch (start us, length us, event | category | flops | bytes accessed | tf_op | source)
XLA Modules:
  0.0 464.9 jit_solution(14369089013032245038)
XLA Ops:
  0.0 1.0 reduce.1
  1.0 0.6 pad_bitcast_fusion
  1.6 0.9 copy.68
  2.6 1.2 reduce.3
  3.7 1.2 reduce.2
  5.1 2.3 fusion.24
  7.6 2.3 convolution_multiply_fusion
  10.3 19.3 %scatter_rows.2 = f32[16,6,16,128]{3,2,1,0:T(8,128)} custom-call(s32[72,128]{1,0:T(8,128)S(1)} %get-tuple-element.5.where_ref, f32[6,72,128]{2,1,0:T(8,128)S(1)} %bitcast.81), custom_call_target="tpu_custom_call" | custom-call | tf_op jit(solution)/shard_map/scatter_rows/pallas_call | solution.py:253
  29.6 8.3 %all-to-all-start = ((f32[16,6,16,128]{3,2,1,0:T(8,128)}), f32[16,6,16,128]{3,2,1,0:T(8,128)S(1)}, u32[]{:S(2)}, u32[]{:S(2)}) async-start(f32[16,6,16,128]{3,2,1,0:T(8,128)} %scatter_rows.2), calls=%async_computation | async-start | bytes 1572864 | tf_op jit(solution)/shard_map/all_to_all | solution.py:407
  38.1 19.6 %all-to-all-done.table_ref = f32[16,6,16,128]{3,2,1,0:T(8,128)S(1)} async-done(((f32[16,6,16,128]{3,2,1,0:T(8,128)}), f32[16,6,16,128]{3,2,1,0:T(8,128)S(1)}, u32[]{:S(2)}, u32[]{:S(2)}) %all-to-all-start) | async-done | bytes 786464 | tf_op jit(solution)/shard_map/all_to_all | solution.py:407
  57.7 0.9 copy-done.3
  58.6 88.5 %gather_rows.2.tiles_ref = f32[256,8,128]{2,1,0:T(8,128)S(1)} custom-call(s32[256,128]{1,0:T(8,128)S(1)} %bitcast.82, f32[16,6,16,128]{3,2,1,0:T(8,128)S(1)} %all-to-all-done.table_ref), custom_call_target="tpu_custom_call" | custom-call | tf_op jit(solution)/shard_map/gather_rows/pallas_call | solution.py:301
  147.1 49.8 %check_values.1 = f32[3,256,128]{2,1,0:T(8,128)S(1)} custom-call(f32[3,256]{1,0:T(4,128)S(1)} %bitcast.85, f32[256,8,128]{2,1,0:T(8,128)S(1)} %gather_rows.2.tiles_ref, f32[8,128]{1,0:T(8,128)S(1)} %pad.22.surface_ref), custom_call_target="tpu_custom_call" | custom-call | tf_op jit(solution)/shard_map/check_values/pallas_call | solution.py:162
  197.0 1.0 copy-done.1
  198.1 0.5 convolution_bitcast_fusion.1
  198.8 2.0 convolution_bitcast_fusion.4
  200.9 1.1 collective-permute-done.2
  202.0 0.6 collective-permute-start.3
  202.6 3.0 collective-permute-done.3
  205.7 1.7 collective-permute-start.4
  207.4 2.0 collective-permute-done.4
  209.4 2.2 collective-permute-start.5
  211.6 0.6 broadcast_clamp_fusion
  212.2 1.0 collective-permute-done.5
  213.2 1.6 collective-permute-start.6
  214.8 0.8 copy.25
  215.6 1.4 collective-permute-start.1
  217.0 4.6 collective-permute-start
  221.6 1.3 collective-permute-start.8
  222.9 5.9 %collective-permute-start.7 = (f32[256,8,128]{2,1,0:T(8,128)}, f32[256,8,128]{2,1,0:T(8,128)}, u32[]{:S(2)}, u32[]{:S(2)}) collective-permute-start(f32[256,8,128]{2,1,0:T(8,128)} %copy-done.1), channel_id=1, source_target_pairs={{0,2},{2,4},{4,6},{6,8},{8,10},{10,12},{12,14},{14,16},{16,18},{18... | collective-permute-start | bytes 3145736 | tf_op jit(solution)/shard_map/ppermute | solution.py:29
  228.8 0.3 convolution_bitcast_fusion.2
  229.1 1.3 convolution_bitcast_fusion.3
  230.3 1.2 fusion.25
  231.6 0.8 copy.32
  232.4 15.3 %collective-permute-done = f32[168,256]{1,0:T(8,128)S(1)} collective-permute-done((f32[168,256]{1,0:T(8,128)S(1)}, f32[168,256]{1,0:T(8,128)S(1)}, u32[]{:S(2)}, u32[]{:S(2)}) %collective-permute-start) | collective-permute-done | bytes 172064 | tf_op jit(solution)/shard_map/ppermute | solution.py:29
  247.7 0.8 pad_maximum_fusion.1
  248.5 1.3 copy.27
  249.8 9.5 %gather_fusion = f32[2048,168]{1,0:T(8,128)} fusion(f32[168,768]{0,1:T(8,128)S(1)} %copy.27, s32[2048]{0:T(1024)} %broadcast_clamp_fusion), kind=kCustom, calls=%fused_computation | custom fusion | bytes 2760704 | tf_op jit(solution)/shard_map/gather | solution.py:356
  259.3 5.0 %convolution_bitcast_fusion = f32[16,168,256]{1,0,2:T(8,128)S(1)} fusion(f32[8,256,168]{2,1,0:T(8,128)} %bitcast.88, s32[8,256]{0,1:T(8,128)} %copy.25), kind=kOutput, calls=%fused_computation.4 | convolution fusion | flops 66093056 | bytes 4136960 | tf_op jit(solution)/shard_map/ejn,jnk->ken/dot_general | solution.py:358
  264.4 8.1 %fusion.7 = f32[168,256]{1,0:T(8,128)S(1)} fusion(f32[168,256]{1,0:T(8,128)S(1)} %copy-done.7, f32[16,168,168]{2,1,0:T(8,128)S(1)} %copy-done, f32[16,168,256]{1,0,2:T(8,128)S(1)} %convolution_bitcast_fusion), kind=kOutput, calls=%fused_computation.10 | convolution fusion | flops 1387309056 | bytes 4902912 | tf_op jit(solution)/shard_map/kef,ken->fn/dot_general | solution.py:359
  272.5 0.2 copy.33
  272.7 2.1 pad_maximum_fusion.tiles_ref
  274.8 68.5 %near_field.1.near_ref = f32[3,256,128]{2,1,0:T(8,128)S(1)} custom-call(f32[3,256]{1,0:T(4,128)S(1)} %bitcast.86, s32[3,256]{1,0:T(4,128)S(1)} %fusion.22.index_ref, f32[768,8,128]{2,1,0:T(8,128)S(1)} %pad_maximum_fusion.tiles_ref), custom_call_target="tpu_custom_call" | custom-call | tf_op jit(solution)/shard_map/near_field/pallas_call | solution.py:137
  343.4 49.8 %far_field.1.value_ref = f32[3,256,128]{2,1,0:T(8,128)S(1)} custom-call(f32[3,256]{1,0:T(4,128)S(1)} %bitcast.87, f32[256,8,128]{2,1,0:T(8,128)S(1)} %copy-done.2, f32[8,128]{1,0:T(8,128)S(1)} %pad.22.surface_ref, f32[3,256,128]{2,1,0:T(8,128)S(1)} %pad.23.local_ref, f32[3,256,128]{2,1,0:T(8,128)S(1)} %near_field.1.near_ref), custom_call_target="tpu_custom_call" | custom-call | tf_op jit(solution)/shard_map/far_field/pallas_call | solution.py:192
  393.2 38.8 %scatter_rows.3 = f32[16,3,16,128]{3,2,1,0:T(8,128)S(1)} custom-call(s32[256,128]{1,0:T(8,128)S(1)} %bitcast.83, f32[3,256,128]{2,1,0:T(8,128)S(1)} %far_field.1.value_ref), custom_call_target="tpu_custom_call" | custom-call | tf_op jit(solution)/shard_map/scatter_rows/pallas_call | solution.py:253
  431.9 14.7 %all_to_all.10.table_ref = f32[16,3,16,128]{3,2,1,0:T(8,128)S(1)} all-to-all(f32[16,3,16,128]{3,2,1,0:T(8,128)S(1)} %scatter_rows.3), channel_id=1, replica_groups=mesh['gx'=16,'gy'=2] {'gx'}, dimensions={0} | all-to-all | bytes 786432 | tf_op jit(solution)/shard_map/all_to_all | solution.py:427
  446.6 17.4 %gather_rows.3 = f32[3,72,128]{2,1,0:T(8,128)S(1)} custom-call(s32[72,128]{1,0:T(8,128)S(1)} %copy-done.5, f32[16,3,16,128]{3,2,1,0:T(8,128)S(1)} %all_to_all.10.table_ref), custom_call_target="tpu_custom_call" | custom-call | tf_op jit(solution)/shard_map/gather_rows/pallas_call | solution.py:301
  464.1 0.7 reshape.151
  (61 shorter events, 1.5 us)
Async XLA Ops:
  0.0 229.0 %copy-start = (f32[16,168,168]{2,1,0:T(8,128)S(1)}, f32[16,168,168]{2,1,0:T(8,128)}, u32[]{:S(2)}) copy-start(f32[16,168,168]{2,1,0:T(8,128)} %param.26) | copy-start | bytes 5419012
  10.0 27.9 %copy-start.11 = (f32[3,1,256]{2,1,0:T(1,128)S(1)}, f32[3,1,256]{2,1,0:T(1,128)}, u32[]{:S(2)}) copy-start(f32[3,1,256]{2,1,0:T(1,128)} %param.19) | copy-start | bytes 9220
  29.6 28.1 %all-to-all-start = ((f32[16,6,16,128]{3,2,1,0:T(8,128)}), f32[16,6,16,128]{3,2,1,0:T(8,128)S(1)}, u32[]{:S(2)}, u32[]{:S(2)}) async-start(f32[16,6,16,128]{3,2,1,0:T(8,128)} %scatter_rows.2), calls=%async_computation | async-start | bytes 1572864 | tf_op jit(solution)/shard_map/all_to_all | solution.py:407
  57.7 0.9 copy-start.3
  147.1 51.0 %copy-start.8 = (f32[168,168]{1,0:T(8,128)S(1)}, f32[168,168]{1,0:T(8,128)}, u32[]{:S(2)}) copy-start(f32[168,168]{1,0:T(8,128)} %param.25) | copy-start | bytes 338692
  196.9 1.0 copy-start.1
  197.9 9.4 %copy-start.10 = (s32[1,8,256]{2,1,0:T(8,128)S(1)}, s32[1,8,256]{2,1,0:T(8,128)}, u32[]{:S(2)}) copy-start(s32[1,8,256]{2,1,0:T(8,128)} %param.22) | copy-start | bytes 24580
  197.9 16.9 %copy-start.12 = (s32[1,3,256]{2,0,1:T(1,128)S(1)}, s32[1,3,256]{2,0,1:T(1,128)}, u32[]{:S(2)}) copy-start(s32[1,3,256]{2,0,1:T(1,128)} %param.21) | copy-start | bytes 9220
  197.9 16.9 %copy-start.9 = (s32[1,8,256]{2,1,0:T(8,128)S(1)}, s32[1,8,256]{2,1,0:T(8,128)}, u32[]{:S(2)}) copy-start(s32[1,8,256]{2,1,0:T(8,128)} %param.23) | copy-start | bytes 24580
  197.9 30.9 %copy-start.13 = (s32[1,1,32]{2,1,0:T(1,128)S(1)}, s32[1,1,32]{2,1,0:T(1,128)}, u32[]{:S(2)}) copy-start(s32[1,1,32]{2,1,0:T(1,128)} %param.24) | copy-start | bytes 388
  200.9 1.1 collective-permute-start.2
  202.0 3.7 collective-permute-start.3
  205.7 3.7 collective-permute-start.4
  209.4 3.8 collective-permute-start.5
  213.2 15.6 %collective-permute-start.6 = (f32[16,168]{1,0:T(8,128)S(1)}, f32[16,168]{1,0:T(8,128)S(1)}, u32[]{:S(2)}, u32[]{:S(2)}) collective-permute-start(f32[16,168]{1,0:T(8,128)S(1)} %maximum_select_fusion.2), channel_id=1, source_target_pairs={{0,16},{2,18},{4,20},{6,22},{8,24},{10,26},{12,28},{14,30},{16,0},... | collective-permute-start | bytes 32264 | tf_op jit(solution)/shard_map/ppermute | solution.py:321
  215.6 14.7 %copy-start.6 = (f32[8,168,168]{2,1,0:T(8,128)S(1)}, f32[8,168,168]{2,1,0:T(8,128)}, u32[]{:S(2)}) copy-start(f32[8,168,168]{2,1,0:T(8,128)} %param.27) | copy-start | bytes 2709508
  215.6 16.8 %collective-permute-start.1 = (f32[168,256]{1,0:T(8,128)S(1)}, f32[168,256]{1,0:T(8,128)S(1)}, u32[]{:S(2)}, u32[]{:S(2)}) collective-permute-start(f32[168,256]{1,0:T(8,128)S(1)} %convolution_bitcast_fusion.1), channel_id=1, source_target_pairs={{2,0},{4,2},{6,4},{8,6},{10,8},{12,10},{14,12},{16,14},{18,16},{20... | collective-permute-start | bytes 516104 | tf_op jit(solution)/shard_map/ppermute | solution.py:30
  217.0 30.7 %collective-permute-start = (f32[168,256]{1,0:T(8,128)S(1)}, f32[168,256]{1,0:T(8,128)S(1)}, u32[]{:S(2)}, u32[]{:S(2)}) collective-permute-start(f32[168,256]{1,0:T(8,128)S(1)} %convolution_bitcast_fusion.1), channel_id=1, source_target_pairs={{0,2},{2,4},{4,6},{6,8},{8,10},{10,12},{12,14},{14,16},{16,18},{18... | collective-permute-start | bytes 516104 | tf_op jit(solution)/shard_map/ppermute | solution.py:29
  221.6 51.1 %collective-permute-start.8 = (f32[256,8,128]{2,1,0:T(8,128)}, f32[256,8,128]{2,1,0:T(8,128)}, u32[]{:S(2)}, u32[]{:S(2)}) collective-permute-start(f32[256,8,128]{2,1,0:T(8,128)} %copy-done.1), channel_id=1, source_target_pairs={{2,0},{4,2},{6,4},{8,6},{10,8},{12,10},{14,12},{16,14},{18,16},{20... | collective-permute-start | bytes 3145736 | tf_op jit(solution)/shard_map/ppermute | solution.py:30
  222.9 49.8 %collective-permute-start.7 = (f32[256,8,128]{2,1,0:T(8,128)}, f32[256,8,128]{2,1,0:T(8,128)}, u32[]{:S(2)}, u32[]{:S(2)}) collective-permute-start(f32[256,8,128]{2,1,0:T(8,128)} %copy-done.1), channel_id=1, source_target_pairs={{0,2},{2,4},{4,6},{6,8},{8,10},{10,12},{12,14},{14,16},{16,18},{18... | collective-permute-start | bytes 3145736 | tf_op jit(solution)/shard_map/ppermute | solution.py:29
  259.3 5.1 %copy-start.7 = (f32[168,256]{1,0:T(8,128)S(1)}, f32[168,256]{1,0:T(8,128)}, u32[]{:S(2)}) copy-start(f32[168,256]{1,0:T(8,128)} %copy.32) | copy-start | bytes 516100
  274.8 68.6 %copy-start.2 = (f32[256,8,128]{2,1,0:T(8,128)S(1)}, f32[256,8,128]{2,1,0:T(8,128)}, u32[]{:S(2)}) copy-start(f32[256,8,128]{2,1,0:T(8,128)} %copy-done.1) | copy-start | bytes 3145732
  274.8 118.4 %copy-start.4 = (s32[1,32768]{1,0:T(1,128)S(1)}, s32[1,32768]{1,0:T(1,128)}, u32[]{:S(2)}) copy-start(s32[1,32768]{1,0:T(1,128)} %param.20) | copy-start | bytes 393220
  343.4 103.3 %copy-start.5 = (s32[72,128]{1,0:T(8,128)S(1)}, s32[72,128]{1,0:T(8,128)}, u32[]{:S(2)}) copy-start(s32[72,128]{1,0:T(8,128)} %get-tuple-element.6.where_ref) | copy-start | bytes 110596
